TPU v7x, 32 devices: a whole 2x2x4 slice. The times are simulated.
32 devices in a mesh: groups: 2 (over y), ctx: 4 (over z), head: 2 (over x), user: 2 (over core).
Axes of the slice: x: 2, y: 2, z: 4, core: 2. Of those that a mesh axis runs over, the one named last changes fastest.
Arguments:
- projected: bfloat16 [4, 2048, 8, 4, 128], P(('groups', 'user'), 'ctx', 'head'), parts along dimension 0, may hold values from -6 to 6
- upstream: bfloat16 [4, 2048, 8, 128], P(('groups', 'user'), 'ctx', 'head'), parts along dimension 0, may hold values from -6 to 6
- ips_weight: float32 [4, 2048], P(('groups', 'user')), parts along dimension 0, may hold values from 0.2 to 5
- item_ids: int32 [4, 2048], P(('groups', 'user')), parts along dimension 0, may hold values from 0 to 999
- session_ids: int32 [4, 2048], P(('groups', 'user')), parts along dimension 0, may hold values from 0 to 7, never falling along the last dimension, each value on 1 to 1024 neighbouring positions
- session_blocks: int32 [4, 4, 3], P(('groups', 'user')), parts along dimension 0, may hold values from -1 to 1, as said below
Outputs:
- mixed: bfloat16 [4, 2048, 8, 128], P(('groups', 'user'), 'ctx', 'head'), parts along dimension 0
- proj_grad: bfloat16 [4, 2048, 8, 4, 128], P(('groups', 'user'), 'ctx', 'head'), parts along dimension 0
There are 2 independent parts, one for each index of `groups`. A program takes and returns all parts, laid end to end along the dimension named above; each array names one. Nothing has to cross between parts.
Inputs may be any that keep to these rules, and one draw needn't show every extreme that they name: `session_blocks`: row b lists, in ascending order, distinct blocks below b, and -1 in the remaining slots; row 3 always lists block 1 and never block 2, and row 1 never lists block 0.
All inputs are finite; a program needn't handle non-finite values.
Results may differ from a plain program's by a relative error of at most 0.0056.
Values may be sent and summed in bfloat16 or wider, within the bound.
A program may use at most 128 MiB of HBM per device.

v0:
```python
import jax
import jax.numpy as jnp
from jax import lax
from jax.sharding import PartitionSpec as P

BLOCK = 512


def shifted_2(block, axis, distance):
    devices = range(lax.axis_size(axis))
    route = [(i - distance, i) for i in devices if i - distance in devices]
    return lax.ppermute(block, axis, route)


def pair_scores(queries, keys):
    scale = queries.shape[-1] ** (-0.5)
    return jnp.einsum("ahd,chd->hac", queries, keys, preferred_element_type=jnp.float32) * scale


def attend(queries, keys, values, visible):
    scores = pair_scores(queries, keys)
    probs = jnp.where(visible[None], jax.nn.silu(scores), 0.0).astype(jnp.bfloat16)
    return jnp.einsum("hac,chd->ahd", probs, values, preferred_element_type=jnp.float32)


def attend_back(queries, grad_rows, keys, values, visible):
    scale = queries.shape[-1] ** (-0.5)
    scores = pair_scores(queries, keys)
    sigma = jax.nn.sigmoid(scores)
    probs = jnp.where(visible[None], jax.nn.silu(scores), 0.0).astype(jnp.bfloat16)
    slope = sigma * (1.0 + scores * (1.0 - sigma))
    dprod = jnp.einsum("ahd,chd->hac", grad_rows, values, preferred_element_type=jnp.float32)
    edges = jnp.where(visible[None], dprod * slope, 0.0).astype(jnp.bfloat16)
    grad_q = jnp.einsum("hac,chd->ahd", edges, keys, preferred_element_type=jnp.float32) * scale
    grad_k = jnp.einsum("hac,ahd->chd", edges, queries, preferred_element_type=jnp.float32) * scale
    grad_v = jnp.einsum("hac,ahd->chd", probs, grad_rows, preferred_element_type=jnp.float32)
    return (grad_q, grad_k, grad_v)


def shards(projected, upstream, ips_weight, item_ids, session_ids, session_blocks):
    rows = projected[0]
    count = rows.shape[0]
    heads = rows.shape[1]
    width = rows.shape[3]
    block = BLOCK
    local_blocks = count // block
    ctx_rank = lax.axis_index("ctx")
    first = ctx_rank * local_blocks
    sessions = session_ids[0]
    lists = session_blocks[0]
    gates = rows[:, :, 0]
    queries = rows[:, :, 1].reshape(local_blocks, block, heads, width)
    pairs = rows[:, :, 2:4]
    pair_blocks = pairs.reshape(local_blocks, block, heads, 2, width)
    inner = jnp.arange(block)
    below = inner[None, :] <= inner[:, None]
    everything = jnp.ones((block, block), bool)

    def session_slice(index):
        return lax.dynamic_slice_in_dim(sessions, jnp.maximum(index, 0) * block, block)

    list_rows = []
    local = 0
    glob = first + local
    here = session_slice(glob)
    there = session_slice(glob - 1)
    list_row = lax.dynamic_index_in_dim(lists, glob, 0, keepdims=False)
    prev_listed = jnp.any(list_row == glob - 1)
    own_masks = [below & (here[:, None] == here[None, :])]
    prev_masks = [
        jnp.logical_not(below)
        & (here[:, None] == there[None, :])
        & (glob > 0)
        & jnp.logical_not(prev_listed)
    ]
    list_rows.append(list_row)
    previous = shifted_2(pair_blocks[local_blocks - 1], "ctx", 1)
    prior = [previous] + [pair_blocks[local] for local in range(local_blocks - 1)]
    local = 0
    current = pair_blocks[local]
    total = attend(queries[local], current[:, :, 0], current[:, :, 1], own_masks[local])
    total = total + attend(
        queries[local], prior[local][:, :, 0], prior[local][:, :, 1], prev_masks[local]
    )
    totals = [total]
    piece_blocks = lax.all_gather(pairs, "ctx", axis=0, tiled=True).reshape(
        -1, block, heads, 2, width
    )

    def visit(index, acc):
        chosen = lax.dynamic_index_in_dim(piece_blocks, index, 0, keepdims=False)
        local = 0
        hit = jnp.any(list_rows[local] == index)
        updated = [
            lax.cond(
                hit,
                lambda value, local=local: value
                + attend(queries[local], chosen[:, :, 0], chosen[:, :, 1], everything),
                lambda value: value,
                acc[local],
            )
        ]
        return tuple(updated)

    summed = lax.fori_loop(0, piece_blocks.shape[0], visit, tuple(totals))
    attended = summed[0]
    centre = jnp.mean(attended, -1, keepdims=True)
    shifted = attended - centre
    inv_std = lax.rsqrt(jnp.mean(shifted * shifted, -1, keepdims=True) + 1e-05)
    normed = shifted * inv_std
    gates_f = gates.astype(jnp.float32)
    mixed = (normed * gates_f).astype(jnp.bfloat16)
    weights_row = ips_weight[0]
    items = item_ids[0]
    fresh = jnp.concatenate(
        [(items[1:] != items[:-1]).astype(jnp.float32), jnp.zeros((1,), jnp.float32)]
    )
    scaled = weights_row * fresh * weights_row.shape[0] / jnp.sum(weights_row)
    local_scale = lax.dynamic_slice_in_dim(scaled, ctx_rank * count, count)
    grad_mixed = local_scale[:, None, None] * upstream[0].astype(jnp.float32)
    grad_gates = (grad_mixed * normed).astype(jnp.bfloat16)
    grad_normed = grad_mixed * gates_f
    grad_att = inv_std * (
        grad_normed
        - jnp.mean(grad_normed, -1, keepdims=True)
        - normed * jnp.mean(grad_normed * normed, -1, keepdims=True)
    )
    grad_flat = grad_att.astype(jnp.bfloat16)
    grad_rows = grad_flat.reshape(local_blocks, block, heads, width)
    grad_q = []
    grad_kv = []
    local = 0
    current = pair_blocks[local]
    own_q, own_k, own_v = attend_back(
        queries[local], grad_rows[local], current[:, :, 0], current[:, :, 1], own_masks[local]
    )
    near_q, near_k, near_v = attend_back(
        queries[local],
        grad_rows[local],
        prior[local][:, :, 0],
        prior[local][:, :, 1],
        prev_masks[local],
    )
    grad_q.append(own_q + near_q)
    grad_kv.append(jnp.stack([own_k, own_v], 2))
    backward_prev = jnp.stack([near_k, near_v], 2)
    incoming = shifted_2(backward_prev.astype(jnp.bfloat16), "ctx", -1).astype(jnp.float32)
    grad_kv[local_blocks - 1] = grad_kv[local_blocks - 1] + incoming
    pulled = jnp.stack([rows[:, :, 1], grad_flat], 2)
    piece_pairs = lax.all_gather(pairs, "ctx", axis=0, tiled=True).reshape(
        -1, block, heads, 2, width
    )
    piece_pulled = lax.all_gather(pulled, "ctx", axis=0, tiled=True).reshape(
        -1, block, heads, 2, width
    )

    def visit(index, acc):
        sums, owned = acc
        chosen = lax.dynamic_index_in_dim(piece_pairs, index, 0, keepdims=False)
        asked = lax.dynamic_index_in_dim(piece_pulled, index, 0, keepdims=False)
        target_list = lax.dynamic_index_in_dim(lists, index, 0, keepdims=False)
        local = 0
        hit = jnp.any(list_rows[local] == index)
        new_sums = [
            lax.cond(
                hit,
                lambda value, local=local: value
                + attend_back(
                    queries[local], grad_rows[local], chosen[:, :, 0], chosen[:, :, 1], everything
                )[0],
                lambda value: value,
                sums[local],
            )
        ]
        mine = jnp.any(target_list == first + local)

        def owner_add(value, local=local):
            part_q, part_k, part_v = attend_back(
                asked[:, :, 0],
                asked[:, :, 1],
                pair_blocks[local][:, :, 0],
                pair_blocks[local][:, :, 1],
                everything,
            )
            return value + jnp.stack([part_k, part_v], 2)

        new_owned = [lax.cond(mine, owner_add, lambda value: value, owned[local])]
        return (tuple(new_sums), tuple(new_owned))

    sums, owned = lax.fori_loop(0, piece_pairs.shape[0], visit, (tuple(grad_q), tuple(grad_kv)))
    grad_q = list(sums)
    grad_kv = list(owned)
    grad_q_all = grad_q[0].astype(jnp.bfloat16)
    grad_kv_all = grad_kv[0].astype(jnp.bfloat16)
    result = jnp.concatenate([grad_gates[:, :, None], grad_q_all[:, :, None], grad_kv_all], 2)
    return (mixed[None], result[None])


def solution(mesh):
    placed = (
        P(("groups", "user"), "ctx", "head", None, None),
        P(("groups", "user"), "ctx", "head", None),
        P(("groups", "user"), None),
        P(("groups", "user"), None),
        P(("groups", "user"), None),
        P(("groups", "user"), None, None),
    )
    return jax.shard_map(
        shards,
        mesh=mesh,
        in_specs=placed,
        out_specs=(
            P(("groups", "user"), "ctx", "head", None),
            P(("groups", "user"), "ctx", "head", None, None),
        ),
        check_vma=False,
    )
```

profile of v0, /device:TPU:12, one launch (start us, length us, event | category | flops | bytes accessed | tf_op | source)
XLA Modules:
  0.0 296.6 jit_solution(7141404065452275830)
XLA Ops:
  7.3 2.1 copy.71
  9.4 1.1 slice.88
  10.6 3.5 %collective-permute-start = (bf16[512,4,2,128]{3,0,1,2:T(8,128)(2,1)}, bf16[512,4,2,128]{3,0,1,2:T(8,128)(2,1)S(1)}, u32[]{:S(2)}, u32[]{:S(2)}) collective-permute-start(bf16[512,4,2,128]{3,0,1,2:T(8,128)(2,1)} %slice.88), channel_id=1, source_target_pairs={{0,4},{4,8},{8,12},{1,5},{5,9},{9,13},{2,6},{6,10},{10,14},{3,7},{... | collective-permute-start | bytes 3145736 | tf_op jit(solution)/shard_map/ppermute | solution.py:12
  14.1 0.9 slice.85
  15.2 0.7 compare_reduce_fusion.4
  17.4 0.8 fusion.71
  18.6 3.6 %select_convert_fusion.3 = (bf16[4,512,512]{2,1,0:T(8,128)(2,1)S(1)}, f32[4,512,512]{2,1,0:T(8,128)}) fusion(pred[512,512]{1,0:T(8,128)(4,1)S(1)} %get-tuple-element.484, bf16[512,4,4,128]{3,0,1,2:T(8,128)(2,1)S(1)} %bitcast.218), kind=kOutput, calls=%fused_computation.64 | convolution fusion | flops 275775488 | bytes 7602176 | tf_op jit(solution)/shard_map/ahd,chd->hac/dot_general | solution.py:17
  22.9 47.2 %collective-permute-done = bf16[512,4,2,128]{3,0,1,2:T(8,128)(2,1)S(1)} collective-permute-done((bf16[512,4,2,128]{3,0,1,2:T(8,128)(2,1)}, bf16[512,4,2,128]{3,0,1,2:T(8,128)(2,1)S(1)}, u32[]{:S(2)}, u32[]{:S(2)}) %collective-permute-start) | collective-permute-done | bytes 1048608 | tf_op jit(solution)/shard_map/ppermute | solution.py:12
  70.1 3.6 %select_convert_fusion.2 = (bf16[4,512,512]{2,1,0:T(8,128)(2,1)S(1)}, f32[4,512,512]{2,1,0:T(8,128)}) fusion(pred[512,512]{1,0:T(8,128)(4,1)S(1)} %get-tuple-element.483, bf16[512,4,2,128]{3,0,1,2:T(8,128)(2,1)S(1)} %collective-permute-done, bf16[512,4,4,128]{3,0,1,2:T(8,128)(2,1)S(1)} %bitcast.220), kind=kOutput, calls=%fused_computation.62 | convolution fusion | flops 275775488 | bytes 7602176 | tf_op jit(solution)/shard_map/ahd,chd->hac/dot_general | solution.py:17
  73.7 1.3 copy-done.7
  75.0 0.7 fusion.47
  75.7 30.0 %all-gather.3.cloned.1.call-done = bf16[2048,4,2,128]{3,0,1,2:T(8,128)(2,1)} async-done(((bf16[512,4,2,128]{3,0,1,2:T(8,128)(2,1)}), bf16[2048,4,2,128]{3,0,1,2:T(8,128)(2,1)}) %all-gather.3.cloned.1.call-update) | async-done | bytes 4194320 | tf_op jit(solution)/shard_map/all_gather | solution.py:86
  105.8 4.6 %copy.34 = bf16[4,512,4,2,128]{4,1,2,3,0:T(8,128)(2,1)} copy(bf16[4,512,4,2,128]{4,1,0,2,3:T(8,128)(2,1)} %bitcast.228) | data formatting | bytes 8388608 | tf_op jit(solution)/shard_map/while | solution.py:105
  110.3 5.4 %while.37 = (s32[]{:T(128)}, f32[512,4,128]{2,0,1:T(8,128)S(1)}, s32[3]{0:T(128)S(1)}, bf16[4,512,4,2,128]{4,1,2,3,0:T(8,128)(2,1)}, bf16[512,4,1,128]{3,0,1,2:T(8,128)(2,1)}, /*index=5*/s32[]{:T(128)}) while((s32[]{:T(128)}, f32[512,4,128]{2,0,1:T(8,128)S(1)}, s32[3]{0:T(128)S(1)}, bf16[4,512,4,2,128]{4,1,2,3,0:T(8,128)(2,1)}, ...), condition=%wide.region_5.6_spmd, body=%wide.region_1.5_spmd.sunk | while | flops 543424512 | bytes 5767345 | solution.py:105
  116.8 3.1 %fusion.59 = (f32[512,4]{0,1:T(4,128)S(1)}, f32[512,4]{0,1:T(4,128)S(1)}, bf16[512,4,1,128]{3,0,1,2:T(8,128)(2,1)}) fusion(f32[512]{0:T(512)S(1)} %fusion.71, bf16[512,4,4,128]{3,0,1,2:T(8,128)(2,1)} %bitcast.221, bf16[1,512,4,128]{3,2,1,0:T(4,128)(2,1)} %param.17, f32[512,4]{0,1:T(4,128)S(1)} %add_rsqrt_fusion, f32[512,4,128]{2,0,1:T(8,128)S(1)} %get-tuple-element.405, ...), kind=kLoop, calls=%fused_computation.101 | loop fusion | flops 2879488 | bytes 2656256 | tf_op jit(solution)/shard_map/reduce_sum | solution.py:125
  120.0 3.0 %multiply_convert_fusion.5 = (bf16[512,4,128]{2,0,1:T(8,128)(2,1)S(1)}, bf16[1,512,4,128]{3,1,2,0:T(8,128)(2,1)}) fusion(f32[512,4,128]{2,0,1:T(8,128)S(1)} %get-tuple-element.405, f32[512,4]{0,1:T(4,128)S(1)} %get-tuple-element.489, f32[512,4]{0,1:T(4,128)S(1)} %get-tuple-element.490, f32[512]{0:T(512)S(1)} %fusion.71, f32[512,4]{0,1:T(4,128)S(1)} %add_rsqrt_fusion, ...), kind=kLoop, calls=%fused_computation.91 | loop fusion | flops 3407872 | bytes 3180544 | tf_op jit(solution)/shard_map/convert_element_type | solution.py:128
  122.9 0.8 copy-done.3
  123.7 2.2 pad_maximum_fusion.1
  126.0 2.4 copy.44
  128.5 2.2 copy.49
  130.7 1.8 copy.47
  132.5 0.9 fusion.50
  133.5 3.8 %select_convert_fusion = bf16[4,512,512]{2,1,0:T(8,128)(2,1)S(1)} fusion(f32[4,512,512]{2,1,0:T(8,128)} %get-tuple-element.488, bf16[512,4,128]{2,0,1:T(8,128)(2,1)S(1)} %copy-done.4, pred[512,512]{1,0:T(8,128)(4,1)S(1)} %copy-done.14, bf16[512,4,2,128]{3,0,1,2:T(8,128)(2,1)S(1)} %copy-done.12), kind=kOutput, calls=%fused_computation.60 | convolution fusion | flops 279969792 | bytes 7602176 | tf_op jit(solution)/shard_map/ahd,chd->hac/dot_general | solution.py:32
  137.3 0.9 fusion.49
  138.3 2.1 collective-permute-start.1
  140.4 2.2 select_convert_fusion.1
  142.6 0.9 convolution_bitcast_fusion
  143.6 0.9 fusion.44
  144.5 0.7 fusion.68
  145.2 1.7 fusion.46
  146.9 56.4 %collective-permute-done.1 = bf16[512,4,2,128]{3,0,1,2:T(8,128)(2,1)S(1)} collective-permute-done((bf16[512,4,2,128]{3,0,1,2:T(8,128)(2,1)S(1)}, bf16[512,4,2,128]{3,0,1,2:T(8,128)(2,1)S(1)}, u32[]{:S(2)}, u32[]{:S(2)}) %collective-permute-start.1) | collective-permute-done | bytes 1048608 | tf_op jit(solution)/shard_map/ppermute | solution.py:12
  203.6 32.4 %all-gather.5.cloned.1.call-done = bf16[2048,4,2,128]{3,0,1,2:T(8,128)(2,1)} async-done(((bf16[512,4,2,128]{3,0,1,2:T(8,128)(2,1)}), bf16[2048,4,2,128]{3,0,1,2:T(8,128)(2,1)}) %all-gather.5.cloned.1.call-update) | async-done | bytes 4194320 | tf_op jit(solution)/shard_map/all_gather | solution.py:153
  236.0 4.6 %copy.45 = bf16[4,512,4,2,128]{4,1,2,3,0:T(8,128)(2,1)} copy(bf16[4,512,4,2,128]{4,1,0,2,3:T(8,128)(2,1)} %bitcast.229) | data formatting | bytes 8388608 | tf_op jit(solution)/shard_map/while | solution.py:190
  240.6 40.9 %while.38 = (s32[]{:T(128)}, f32[512,4,128]{2,0,1:T(8,128)}, f32[512,4,2,128]{3,0,1,2:T(8,128)S(1)}, s32[3]{0:T(128)S(1)}, bf16[4,512,4,2,128]{4,1,2,3,0:T(8,128...) while((s32[]{:T(128)}, f32[512,4,128]{2,0,1:T(8,128)}, ...), condition=%wide.region_18.19_spmd, body=%wide.region_11.18_spmd.sunk | while | flops 1908146176 | bytes 45613352 | solution.py:190
  248.5 15.1 %conditional.8 = (f32[512,4,2,128]{3,0,1,2:T(8,128)S(1)}) conditional(s32[]{:T(128)} %convert_element_type.150, f32[512,4,2,128]{3,0,1,2:T(8,128)S(1)} %get-tuple-element.621, (bf16[4,512,4,2,128]{4,1,2,3,0:T(8,128)(2,1)}, s32[]{:T(128)}, bf16[512,4,2,128]{3,0,1,2:T(8,128)(2,1)}, f32[512,4,2,128]{3,0,1,2:T(8,128)S(1)}) %tuple.114), branch_computations={%region_16.16_spmd, %region_17.17_spmd} | conditional | flops 1091829760 | bytes 30408744 | solution.py:187
  248.5 1.3 dynamic-slice_bitcast_fusion.2
  249.9 3.7 %fusion.33 = f32[4,512,512]{2,1,0:T(8,128)} fusion(bf16[512,4,2,128]{3,0,1,2:T(8,128)(2,1)} %get-tuple-element.387, bf16[512,4,2,128]{3,0,1,2:T(8,128)(2,1)S(1)} %dynamic-slice_bitcast_fusion.2), kind=kOutput, calls=%fused_computation.49 | convolution fusion | flops 268435456 | bytes 5242880 | tf_op jit(solution)/shard_map/while/body/eval_jaxpr/cond/branch_1_fun/ahd,chd->hac/dot_general | solution.py:17
  253.6 5.7 %fusion.32 = f32[512,4,1,128]{3,0,1,2:T(8,128)} fusion(f32[4,512,512]{2,1,0:T(8,128)} %fusion.33, bf16[512,4,2,128]{3,0,1,2:T(8,128)(2,1)} %get-tuple-element.387, bf16[512,4,2,128]{3,0,1,2:T(8,128)(2,1)S(1)} %dynamic-slice_bitcast_fusion.2), kind=kOutput, calls=%fused_computation.45 | convolution fusion | flops 547618816 | bytes 6815744 | tf_op jit(solution)/shard_map/while/body/eval_jaxpr/cond/branch_1_fun/hac,ahd->chd/dot_general | solution.py:35
  259.3 3.8 %fusion.30 = f32[512,4,1,128]{3,0,1,2:T(8,128)S(1)} fusion(f32[4,512,512]{2,1,0:T(8,128)} %fusion.33, bf16[512,4,2,128]{3,0,1,2:T(8,128)(2,1)S(1)} %dynamic-slice_bitcast_fusion.2), kind=kOutput, calls=%fused_computation.43 | convolution fusion | flops 274726912 | bytes 5767168 | tf_op jit(solution)/shard_map/while/body/eval_jaxpr/cond/branch_1_fun/hac,ahd->chd/dot_general | solution.py:36
  266.3 15.1 %conditional.8 = (f32[512,4,2,128]{3,0,1,2:T(8,128)S(1)}) conditional(s32[]{:T(128)} %convert_element_type.150, f32[512,4,2,128]{3,0,1,2:T(8,128)S(1)} %get-tuple-element.621, (bf16[4,512,4,2,128]{4,1,2,3,0:T(8,128)(2,1)}, s32[]{:T(128)}, bf16[512,4,2,128]{3,0,1,2:T(8,128)(2,1)}, f32[512,4,2,128]{3,0,1,2:T(8,128)S(1)}) %tuple.114), branch_computations={%region_16.16_spmd, %region_17.17_spmd} | conditional | flops 1091829760 | bytes 30408744 | solution.py:187
  266.3 1.3 dynamic-slice_bitcast_fusion.2
  267.6 3.7 %fusion.33 = f32[4,512,512]{2,1,0:T(8,128)} fusion(bf16[512,4,2,128]{3,0,1,2:T(8,128)(2,1)} %get-tuple-element.387, bf16[512,4,2,128]{3,0,1,2:T(8,128)(2,1)S(1)} %dynamic-slice_bitcast_fusion.2), kind=kOutput, calls=%fused_computation.49 | convolution fusion | flops 268435456 | bytes 5242880 | tf_op jit(solution)/shard_map/while/body/eval_jaxpr/cond/branch_1_fun/ahd,chd->hac/dot_general | solution.py:17
  271.3 5.7 %fusion.32 = f32[512,4,1,128]{3,0,1,2:T(8,128)} fusion(f32[4,512,512]{2,1,0:T(8,128)} %fusion.33, bf16[512,4,2,128]{3,0,1,2:T(8,128)(2,1)} %get-tuple-element.387, bf16[512,4,2,128]{3,0,1,2:T(8,128)(2,1)S(1)} %dynamic-slice_bitcast_fusion.2), kind=kOutput, calls=%fused_computation.45 | convolution fusion | flops 547618816 | bytes 6815744 | tf_op jit(solution)/shard_map/while/body/eval_jaxpr/cond/branch_1_fun/hac,ahd->chd/dot_general | solution.py:35
  277.0 3.8 %fusion.30 = f32[512,4,1,128]{3,0,1,2:T(8,128)S(1)} fusion(f32[4,512,512]{2,1,0:T(8,128)} %fusion.33, bf16[512,4,2,128]{3,0,1,2:T(8,128)(2,1)S(1)} %dynamic-slice_bitcast_fusion.2), kind=kOutput, calls=%fused_computation.43 | convolution fusion | flops 274726912 | bytes 5767168 | tf_op jit(solution)/shard_map/while/body/eval_jaxpr/cond/branch_1_fun/hac,ahd->chd/dot_general | solution.py:36
  281.4 1.6 copy.70
  283.1 1.3 convert_bitcast_fusion
  284.4 0.8 copy.48
  285.2 4.5 %maximum_bitcast_fusion = bf16[1,512,4,4,128]{4,3,2,1,0:T(4,128)(2,1)} fusion(bf16[512,4,2,128]{3,2,1,0:T(2,128)(2,1)S(1)} %copy.70, bf16[512,4,1,128]{3,2,1,0:T(2,128)(2,1)S(1)} %copy.48, bf16[512,4,1,128]{3,2,1,0:T(2,128)(2,1)S(1)} %copy-done.9), kind=kLoop, calls=%fused_computation.67 | loop fusion | flops 6291456 | bytes 4194304 | tf_op jit(solution)/shard_map/broadcast_in_dim | solution.py:196
  (82 shorter events, 13.1 us)
Async XLA Ops:
  7.2 7.8 %copy-start.17 = (s32[1,4,3]{1,0,2:T(1,128)S(1)}, s32[1,4,3]{1,0,2:T(1,128)}, u32[]{:S(2)}) copy-start(s32[1,4,3]{1,0,2:T(1,128)} %param.21) | copy-start | bytes 148
  7.2 9.5 %copy-start.16 = (f32[1,2048]{1,0:T(1,128)S(1)}, f32[1,2048]{1,0:T(1,128)}, u32[]{:S(2)}) copy-start(f32[1,2048]{1,0:T(1,128)} %param.18) | copy-start | bytes 24580
  7.2 10.2 %copy-start.15 = (s32[1,2048]{1,0:T(1,128)S(1)}, s32[1,2048]{1,0:T(1,128)}, u32[]{:S(2)}) copy-start(s32[1,2048]{1,0:T(1,128)} %param.19) | copy-start | bytes 24580
  7.2 11.0 %copy-start.18 = (s32[1,2048]{1,0:T(1,128)S(1)}, s32[1,2048]{1,0:T(1,128)}, u32[]{:S(2)}) copy-start(s32[1,2048]{1,0:T(1,128)} %param.20) | copy-start | bytes 24580
  7.2 98.6 %all-gather.3.cloned.1.call-start = ((), (), s32[]{:S(2)}) async-start(), calls=%async_computation | async-start | bytes 5242880 | tf_op jit(solution)/shard_map/all_gather | solution.py:86
  9.4 60.7 %copy-start.1 = (bf16[1,512,4,4,128]{4,1,2,3,0:T(8,128)(2,1)}, bf16[1,512,4,4,128]{4,1,2,3,0:T(8,128)(2,1)S(1)}, u32[]{:S(2)}) copy-start(bf16[1,512,4,4,128]{4,1,2,3,0:T(8,128)(2,1)S(1)} %copy.71) | copy-start | bytes 6291460
  10.6 225.4 %all-gather.5.cloned.1.call-start = ((), (), s32[]{:S(2)}) async-start(), calls=%async_computation.1 | async-start | bytes 5242880 | tf_op jit(solution)/shard_map/all_gather | solution.py:153
  10.6 59.5 %collective-permute-start = (bf16[512,4,2,128]{3,0,1,2:T(8,128)(2,1)}, bf16[512,4,2,128]{3,0,1,2:T(8,128)(2,1)S(1)}, u32[]{:S(2)}, u32[]{:S(2)}) collective-permute-start(bf16[512,4,2,128]{3,0,1,2:T(8,128)(2,1)} %slice.88), channel_id=1, source_target_pairs={{0,4},{4,8},{8,12},{1,5},{5,9},{9,13},{2,6},{6,10},{10,14},{3,7},{... | collective-permute-start | bytes 3145736 | tf_op jit(solution)/shard_map/ppermute | solution.py:12
  18.6 51.5 %copy-start.13 = (pred[512,512]{1,0:T(8,128)(4,1)}, pred[512,512]{1,0:T(8,128)(4,1)S(1)}, u32[]{:S(2)}) copy-start(pred[512,512]{1,0:T(8,128)(4,1)S(1)} %get-tuple-element.483) | copy-start | bytes 786436
  22.2 51.5 %copy-start.5 = (bf16[4,512,512]{2,1,0:T(8,128)(2,1)}, bf16[4,512,512]{2,1,0:T(8,128)(2,1)S(1)}, u32[]{:S(2)}) copy-start(bf16[4,512,512]{2,1,0:T(8,128)(2,1)S(1)} %get-tuple-element.485) | copy-start | bytes 6291460
  70.1 3.6 %copy-start.11 = (bf16[512,4,2,128]{3,0,1,2:T(8,128)(2,1)}, bf16[512,4,2,128]{3,0,1,2:T(8,128)(2,1)S(1)}, u32[]{:S(2)}) copy-start(bf16[512,4,2,128]{3,0,1,2:T(8,128)(2,1)S(1)} %collective-permute-done) | copy-start | bytes 3145732
  73.7 1.3 copy-start.7
  115.8 4.2 %copy-start.2 = (bf16[1,512,4,4,128]{4,1,2,3,0:T(8,128)(2,1)S(1)}, bf16[1,512,4,4,128]{4,1,2,3,0:T(8,128)(2,1)}, u32[]{:S(2)}) copy-start(bf16[1,512,4,4,128]{4,1,2,3,0:T(8,128)(2,1)} %copy-done.1) | copy-start | bytes 6291460
  122.9 0.8 copy-start.3
  122.9 7.8 %copy-start.10 = (bf16[512,4,1,128]{3,0,1,2:T(8,128)(2,1)S(1)}, bf16[512,4,1,128]{3,0,1,2:T(8,128)(2,1)}, u32[]{:S(2)}) copy-start(bf16[512,4,1,128]{3,0,1,2:T(8,128)(2,1)} %get-tuple-element.480) | copy-start | bytes 1572868
  125.9 6.6 %copy-start.4 = (bf16[512,4,128]{2,0,1:T(8,128)(2,1)S(1)}, bf16[512,4,128]{2,0,1:T(8,128)(2,1)}, u32[]{:S(2)}) copy-start(bf16[512,4,128]{2,0,1:T(8,128)(2,1)} %copy-done.3) | copy-start | bytes 1572868
  126.0 6.5 %copy-start.8 = (bf16[4,512,512]{2,1,0:T(8,128)(2,1)S(1)}, bf16[4,512,512]{2,1,0:T(8,128)(2,1)}, u32[]{:S(2)}) copy-start(bf16[4,512,512]{2,1,0:T(8,128)(2,1)} %copy-done.7) | copy-start | bytes 6291460
  126.0 7.4 %copy-start.12 = (bf16[512,4,2,128]{3,0,1,2:T(8,128)(2,1)S(1)}, bf16[512,4,2,128]{3,0,1,2:T(8,128)(2,1)}, u32[]{:S(2)}) copy-start(bf16[512,4,2,128]{3,0,1,2:T(8,128)(2,1)} %copy-done.11) | copy-start | bytes 3145732
  126.0 7.4 %copy-start.14 = (pred[512,512]{1,0:T(8,128)(4,1)S(1)}, pred[512,512]{1,0:T(8,128)(4,1)}, u32[]{:S(2)}) copy-start(pred[512,512]{1,0:T(8,128)(4,1)} %copy-done.13) | copy-start | bytes 786436
  137.3 3.1 %copy-start.19 = (f32[4,512,512]{2,1,0:T(8,128)S(1)}, f32[4,512,512]{2,1,0:T(8,128)}, u32[]{:S(2)}) copy-start(f32[4,512,512]{2,1,0:T(8,128)} %get-tuple-element.486) | copy-start | bytes 12582916
  138.3 65.0 %collective-permute-start.1 = (bf16[512,4,2,128]{3,0,1,2:T(8,128)(2,1)S(1)}, bf16[512,4,2,128]{3,0,1,2:T(8,128)(2,1)S(1)}, u32[]{:S(2)}, u32[]{:S(2)}) collective-permute-start(bf16[512,4,2,128]{3,0,1,2:T(8,128)(2,1)S(1)} %pad_maximum_fusion), channel_id=1, source_target_pairs={{4,0},{8,4},{12,8},{5,1},{9,5},{13,9},{6,2},{10,6},{14,10},{7,3},{... | collective-permute-start | bytes 3145736 | tf_op jit(solution)/shard_map/ppermute | solution.py:12
  140.4 2.3 copy-start.6
  259.3 3.8 %copy-start = (f32[512,4,1,128]{3,0,1,2:T(8,128)S(1)}, f32[512,4,1,128]{3,0,1,2:T(8,128)}, u32[]{:S(2)}) copy-start(f32[512,4,1,128]{3,0,1,2:T(8,128)} %fusion.32) | copy-start | bytes 3145732 | tf_op jit(solution)/shard_map/while/body/eval_jaxpr/cond
  277.0 3.8 %copy-start = (f32[512,4,1,128]{3,0,1,2:T(8,128)S(1)}, f32[512,4,1,128]{3,0,1,2:T(8,128)}, u32[]{:S(2)}) copy-start(f32[512,4,1,128]{3,0,1,2:T(8,128)} %fusion.32) | copy-start | bytes 3145732 | tf_op jit(solution)/shard_map/while/body/eval_jaxpr/cond
  281.4 3.8 %copy-start.9 = (bf16[512,4,1,128]{3,2,1,0:T(2,128)(2,1)S(1)}, bf16[512,4,1,128]{3,2,1,0:T(2,128)(2,1)}, u32[]{:S(2)}) copy-start(bf16[512,4,1,128]{3,2,1,0:T(2,128)(2,1)} %copy.47) | copy-start | bytes 1572868
Sparse Core Ops, SparseCore 0:
  10.7 95.0 all-gather.2
  126.0 109.8 all-gather.4
where the time goes:
time: 297 us
  waiting for transfers between devices  166 us (56%)
  matrix products  47.1 us (16%)
  local copies, waits for them, and re-layouts  27.4 us (9%)
  other arithmetic  27.3 us (9%)
  between operations  15 us (5%)
  loops' own time  8.06 us (3%)
  starting transfers between devices  5.62 us (2%)
    ppermute x2, waiting for transfers between devices, shifted_2(): return lax.ppermute(block, axis, route)  104 us
    all_gather x1, waiting for transfers between devices, shards(): lax.all_gather(pulled, 'ctx', axis=0, tiled=True)  32.4 us
    all_gather x1, waiting for transfers between devices, shards(): lax.all_gather(pairs, 'ctx', axis=0, tiled=True)  30 us
    dot_general x4, matrix products, pair_scores(): jnp.einsum('ahd,chd->hac', queries, keys, preferred_element_type=jnp.floa...  14.6 us
    dot_general x4, matrix products, attend_back(): jnp.einsum('hac,ahd->chd', edges, queries, preferred_element_type=jnp.flo...  13.3 us
    dot_general x4, matrix products, attend_back(): jnp.einsum('hac,ahd->chd', probs, grad_rows, preferred_element_type=jnp.f...  9.46 us
    while x3, local copies, waits for them, and re-layouts, shards(): lax.fori_loop(0, piece_pairs.shape[0], visit, (tuple(grad_q), tuple(grad_...  8.68 us
    unnamed x41, local copies, waits for them, and re-layouts  6.66 us
  transfers between devices with their start and end apart: 4, of which 4 were waited for; matrix products, arithmetic and copies ran while one was open for 11% of the time, Pallas kernels for 0%

commit v1 on v0

--- a/solution.py
+++ b/solution.py
@@ -4,6 +4,18 @@
 from jax.sharding import PartitionSpec as P
 
 BLOCK = 512
+
+
+def ring_gather(value, axis, dim):
+    ways, here, step = (lax.axis_size(axis), lax.axis_index(axis), value.shape[dim])
+    dims = [n * ways if d == dim else n for d, n in enumerate(value.shape)]
+    full = lax.dynamic_update_slice_in_dim(
+        jnp.zeros(dims, value.dtype), value, here * step, axis=dim
+    )
+    for far in range(1, ways):
+        value = lax.ppermute(value, axis, [(d, (d + 1) % ways) for d in range(ways)])
+        full = lax.dynamic_update_slice_in_dim(full, value, (here - far) % ways * step, axis=dim)
+    return full
 
 
 def shifted_2(block, axis, distance):
@@ -150,9 +162,7 @@
     piece_pairs = lax.all_gather(pairs, "ctx", axis=0, tiled=True).reshape(
         -1, block, heads, 2, width
     )
-    piece_pulled = lax.all_gather(pulled, "ctx", axis=0, tiled=True).reshape(
-        -1, block, heads, 2, width
-    )
+    piece_pulled = ring_gather(pulled, "ctx", 0).reshape(-1, block, heads, 2, width)
 
     def visit(index, acc):
         sums, owned = acc

time: 297 us -> 288 us (0.970)
  waiting for transfers between devices: 166 us -> 153 us
  starting transfers between devices: 5.62 us -> 15.2 us
  matrix products: 47.1 us -> 43.4 us
    ppermute x0 -> x3, waiting for transfers between devices: none -> 77.2 us  [ring_gather(): lax.ppermute(value, axis, [(d, (d + 1) % ways) for d in range(ways)])]
    ppermute x2, waiting for transfers between devices: 104 us -> 48 us  [shifted_2(): return lax.ppermute(block, axis, route)]
    all_gather x1 -> x0, waiting for transfers between devices: 32.4 us -> none  [shards(): lax.all_gather(pulled, 'ctx', axis=0, tiled=True)]
    ppermute x0 -> x3, starting transfers between devices: none -> 9.8 us  [ring_gather(): lax.ppermute(value, axis, [(d, (d + 1) % ways) for d in range(ways)])]
    cond x4, local copies, waits for them, and re-layouts: 0.01 us -> 3.9 us
    while x3, local copies, waits for them, and re-layouts: 8.68 us -> 5.08 us  [shards(): lax.fori_loop(0, piece_pairs.shape[0], visit, (tuple(grad_q), tuple(grad_...]
    unnamed x41 -> x37, local copies, waits for them, and re-layouts: 6.66 us -> 4.8 us
  transfers between devices with their start and end apart: 4 -> 6, of which waited for: 4 -> 5; matrix products, arithmetic and copies ran while one was open for 11% -> 9% of each run, Pallas kernels for 0% -> 0%
where the time goes in v1:
time: 288 us; the launch traced here: 287 us
  waiting for transfers between devices  153 us (53%)
  matrix products  43.4 us (15%)
  other arithmetic  26.9 us (9%)
  local copies, waits for them, and re-layouts  25.9 us (9%)
  starting transfers between devices  15.2 us (5%)
  between operations  15.2 us (5%)
  loops' own time  7.24 us (3%)
    ppermute x3, waiting for transfers between devices, ring_gather(): lax.ppermute(value, axis, [(d, (d + 1) % ways) for d in range(ways)])  77.2 us
    ppermute x2, waiting for transfers between devices, shifted_2(): return lax.ppermute(block, axis, route)  48 us
    all_gather x1, waiting for transfers between devices, shards(): lax.all_gather(pairs, 'ctx', axis=0, tiled=True)  28 us
    dot_general x4, matrix products, attend_back(): jnp.einsum('hac,ahd->chd', edges, queries, preferred_element_type=jnp.flo...  13.2 us
    dot_general x4, matrix products, pair_scores(): jnp.einsum('ahd,chd->hac', queries, keys, preferred_element_type=jnp.floa...  11.7 us
    ppermute x3, starting transfers between devices, ring_gather(): lax.ppermute(value, axis, [(d, (d + 1) % ways) for d in range(ways)])  9.8 us
    dot_general x4, matrix products, attend_back(): jnp.einsum('hac,ahd->chd', probs, grad_rows, preferred_element_type=jnp.f...  6.95 us
  transfers between devices with their start and end apart: 6, of which 5 were waited for; matrix products, arithmetic and copies ran while one was open for 9% of the time, Pallas kernels for 0%

profile of v1, /device:TPU:12, one launch (start us, length us, event | category | flops | bytes accessed | tf_op | source)
XLA Modules:
  0.0 287.2 jit_solution(12508565973019763576)
XLA Ops:
  7.2 2.1 copy.78
  9.4 1.1 slice.88
  10.6 3.5 %collective-permute-start = (bf16[512,4,2,128]{3,0,1,2:T(8,128)(2,1)}, bf16[512,4,2,128]{3,0,1,2:T(8,128)(2,1)}, u32[]{:S(2)}, u32[]{:S(2)}) collective-permute-start(bf16[512,4,2,128]{3,0,1,2:T(8,128)(2,1)} %slice.88), channel_id=1, source_target_pairs={{0,4},{4,8},{8,12},{1,5},{5,9},{9,13},{2,6},{6,10},{10,14},{3,7},{... | collective-permute-start | bytes 3145736 | tf_op jit(solution)/shard_map/ppermute | solution.py:24
  17.7 3.6 %select_convert_fusion.3 = (bf16[4,512,512]{2,1,0:T(8,128)(2,1)S(1)}, f32[4,512,512]{2,1,0:T(8,128)}) fusion(pred[512,512]{1,0:T(8,128)(4,1)S(1)} %get-tuple-element.484, bf16[512,4,4,128]{3,0,1,2:T(8,128)(2,1)S(1)} %bitcast.218), kind=kOutput, calls=%fused_computation.64 | convolution fusion | flops 275775488 | bytes 7602176 | tf_op jit(solution)/shard_map/ahd,chd->hac/dot_general | solution.py:29
  22.0 48.0 %collective-permute-done = bf16[512,4,2,128]{3,0,1,2:T(8,128)(2,1)} collective-permute-done((bf16[512,4,2,128]{3,0,1,2:T(8,128)(2,1)}, bf16[512,4,2,128]{3,0,1,2:T(8,128)(2,1)}, u32[]{:S(2)}, u32[]{:S(2)}) %collective-permute-start) | collective-permute-done | bytes 1048608 | tf_op jit(solution)/shard_map/ppermute | solution.py:24
  70.0 4.6 %select_convert_fusion.2 = (bf16[4,512,512]{2,1,0:T(8,128)(2,1)S(1)}, f32[4,512,512]{2,1,0:T(8,128)}) fusion(pred[512,512]{1,0:T(8,128)(4,1)S(1)} %get-tuple-element.483, bf16[512,4,2,128]{3,0,1,2:T(8,128)(2,1)} %collective-permute-done, bf16[512,4,4,128]{3,0,1,2:T(8,128)(2,1)S(1)} %bitcast.220), kind=kOutput, calls=%fused_computation.62 | convolution fusion | flops 275775488 | bytes 7602176 | tf_op jit(solution)/shard_map/ahd,chd->hac/dot_general | solution.py:29
  74.6 1.3 copy-done.6
  75.9 1.8 fusion.47
  77.7 28.0 %all-gather.2.cloned.1.call-done = bf16[2048,4,2,128]{3,0,1,2:T(8,128)(2,1)} async-done(((bf16[512,4,2,128]{3,0,1,2:T(8,128)(2,1)}), bf16[2048,4,2,128]{3,0,1,2:T(8,128)(2,1)}) %all-gather.2.cloned.1.call-update) | async-done | bytes 4194320 | tf_op jit(solution)/shard_map/all_gather | solution.py:98
  105.7 4.6 %copy.33 = bf16[4,512,4,2,128]{4,1,2,3,0:T(8,128)(2,1)} copy(bf16[4,512,4,2,128]{4,1,0,2,3:T(8,128)(2,1)} %bitcast.230) | data formatting | bytes 8388608 | tf_op jit(solution)/shard_map/while | solution.py:117
  110.3 4.8 %while.37 = (s32[]{:T(128)}, f32[512,4,128]{2,0,1:T(8,128)S(1)}, s32[3]{0:T(128)S(1)}, bf16[4,512,4,2,128]{4,1,2,3,0:T(8,128)(2,1)}, bf16[512,4,1,128]{3,0,1,2:T(8,128)(2,1)S(1)}, /*index=5*/s32[]{:T(128)}) while((s32[]{:T(128)}, f32[512,4,128]{2,0,1:T(8,128)S(1)}, s32[3]{0:T(128)S(1)}, bf16[4,512,4,2,128]{4,1,2,3,0:T(8,128)(2,1)}, ...), condition=%wide.region_5.6_spmd, body=%wide.region_1.5_spmd.sunk | while | flops 543424512 | bytes 5767345 | solution.py:117
  116.2 2.5 fusion.59
  118.7 3.0 %multiply_convert_fusion.5 = (bf16[512,4,128]{2,0,1:T(8,128)(2,1)S(1)}, bf16[1,512,4,128]{3,1,2,0:T(8,128)(2,1)S(1)}) fusion(f32[512,4,128]{2,0,1:T(8,128)S(1)} %get-tuple-element.405, f32[512,4]{0,1:T(4,128)S(1)} %get-tuple-element.489, f32[512,4]{0,1:T(4,128)S(1)} %get-tuple-element.490, f32[512]{0:T(512)S(1)} %fusion.71, f32[512,4]{0,1:T(4,128)S(1)} %add_rsqrt_fusion, ...), kind=kLoop, calls=%fused_computation.95 | loop fusion | flops 3407872 | bytes 3180544 | tf_op jit(solution)/shard_map/convert_element_type | solution.py:140
  121.7 0.9 fusion.50
  122.6 3.3 %select_convert_fusion = bf16[4,512,512]{2,1,0:T(8,128)(2,1)S(1)} fusion(f32[4,512,512]{2,1,0:T(8,128)S(1)} %copy-done.17, bf16[512,4,128]{2,0,1:T(8,128)(2,1)S(1)} %get-tuple-element.478, pred[512,512]{1,0:T(8,128)(4,1)S(1)} %copy-done.11, bf16[512,4,2,128]{3,0,1,2:T(8,128)(2,1)} %collective-permute-done), kind=kOutput, calls=%fused_computation.60 | convolution fusion | flops 279969792 | bytes 7602176 | tf_op jit(solution)/shard_map/ahd,chd->hac/dot_general | solution.py:44
  125.9 0.9 fusion.49
  127.0 2.4 collective-permute-start.2
  129.5 1.9 collective-permute-start.1
  131.4 2.2 select_convert_fusion.1
  133.6 18.5 %collective-permute-done.2 = bf16[512,4,2,128]{3,0,1,2:T(8,128)(2,1)S(1)} collective-permute-done((bf16[512,4,2,128]{3,0,1,2:T(8,128)(2,1)S(1)}, bf16[512,4,2,128]{3,0,1,2:T(8,128)(2,1)S(1)}, u32[]{:S(2)}, u32[]{:S(2)}) %collective-permute-start.2) | collective-permute-done | bytes 1048608 | tf_op jit(solution)/shard_map/ppermute | solution.py:16
  152.2 7.4 %collective-permute-start.3 = (bf16[512,4,2,128]{3,0,1,2:T(8,128)(2,1)S(1)}, bf16[512,4,2,128]{3,0,1,2:T(8,128)(2,1)S(1)}, u32[]{:S(2)}, u32[]{:S(2)}) collective-permute-start(bf16[512,4,2,128]{3,0,1,2:T(8,128)(2,1)S(1)} %collective-permute-done.2), channel_id=1, source_target_pairs={{0,4},{4,8},{8,12},{12,0},{1,5},{5,9},{9,13},{13,1},{2,6},{6,10},{... | collective-permute-start | bytes 3145736 | tf_op jit(solution)/shard_map/ppermute | solution.py:16
  160.3 0.9 fusion.44
  161.3 1.2 copy.47
  162.4 1.2 copy.52
  163.6 1.8 copy.50
  166.1 2.9 fusion.46
  169.0 15.2 %collective-permute-done.3 = bf16[512,4,2,128]{3,0,1,2:T(8,128)(2,1)S(1)} collective-permute-done((bf16[512,4,2,128]{3,0,1,2:T(8,128)(2,1)S(1)}, bf16[512,4,2,128]{3,0,1,2:T(8,128)(2,1)S(1)}, u32[]{:S(2)}, u32[]{:S(2)}) %collective-permute-start.3) | collective-permute-done | bytes 1048608 | tf_op jit(solution)/shard_map/ppermute | solution.py:16
  184.2 0.9 convolution_bitcast_fusion
  185.7 43.5 %collective-permute-done.4 = bf16[512,4,2,128]{3,0,1,2:T(8,128)(2,1)S(1)} collective-permute-done((bf16[512,4,2,128]{3,0,1,2:T(8,128)(2,1)S(1)}, bf16[512,4,2,128]{3,0,1,2:T(8,128)(2,1)S(1)}, u32[]{:S(2)}, u32[]{:S(2)}) %collective-permute-start.4) | collective-permute-done | bytes 1048608 | tf_op jit(solution)/shard_map/ppermute | solution.py:16
  229.3 2.3 copy.48
  231.6 40.5 %while.38 = (s32[]{:T(128)}, f32[512,4,128]{2,0,1:T(8,128)}, f32[512,4,2,128]{3,0,1,2:T(8,128)S(1)}, s32[3]{0:T(128)S(1)}, bf16[4,512,4,2,128]{4,1,2,3,0:T(8,128...) while((s32[]{:T(128)}, f32[512,4,128]{2,0,1:T(8,128)}, ...), condition=%wide.region_18.19_spmd, body=%wide.region_11.18_spmd.sunk | while | flops 1908146176 | bytes 58196264 | solution.py:200
  239.0 15.3 %conditional.8 = (f32[512,4,2,128]{3,0,1,2:T(8,128)S(1)}) conditional(s32[]{:T(128)} %convert_element_type.150, f32[512,4,2,128]{3,0,1,2:T(8,128)S(1)} %get-tuple-element.621, (bf16[4,512,4,2,128]{4,1,2,3,0:T(8,128)(2,1)}, s32[]{:T(128)}, bf16[512,4,2,128]{3,0,1,2:T(8,128)(2,1)}, f32[512,4,2,128]{3,0,1,2:T(8,128)S(1)}) %tuple.114), branch_computations={%region_16.16_spmd, %region_17.17_spmd} | conditional | flops 1091829760 | bytes 42991656 | solution.py:197
  239.0 1.3 dynamic-slice_bitcast_fusion.2
  240.3 1.7 fusion.33
  242.1 1.9 copy-done
  244.0 2.6 fusion.30
  246.6 5.7 %fusion.32 = f32[512,4,1,128]{3,0,1,2:T(8,128)} fusion(f32[4,512,512]{2,1,0:T(8,128)} %copy-done, bf16[512,4,2,128]{3,0,1,2:T(8,128)(2,1)} %get-tuple-element.387, bf16[512,4,2,128]{3,0,1,2:T(8,128)(2,1)S(1)} %dynamic-slice_bitcast_fusion.2), kind=kOutput, calls=%fused_computation.45 | convolution fusion | flops 547618816 | bytes 6815744 | tf_op jit(solution)/shard_map/while/body/eval_jaxpr/cond/branch_1_fun/hac,ahd->chd/dot_general | solution.py:47
  252.3 2.0 maximum_add_fusion
  256.8 15.3 %conditional.8 = (f32[512,4,2,128]{3,0,1,2:T(8,128)S(1)}) conditional(s32[]{:T(128)} %convert_element_type.150, f32[512,4,2,128]{3,0,1,2:T(8,128)S(1)} %get-tuple-element.621, (bf16[4,512,4,2,128]{4,1,2,3,0:T(8,128)(2,1)}, s32[]{:T(128)}, bf16[512,4,2,128]{3,0,1,2:T(8,128)(2,1)}, f32[512,4,2,128]{3,0,1,2:T(8,128)S(1)}) %tuple.114), branch_computations={%region_16.16_spmd, %region_17.17_spmd} | conditional | flops 1091829760 | bytes 42991656 | solution.py:197
  256.8 1.3 dynamic-slice_bitcast_fusion.2
  258.1 1.7 fusion.33
  259.9 1.9 copy-done
  261.8 2.6 fusion.30
  264.4 5.7 %fusion.32 = f32[512,4,1,128]{3,0,1,2:T(8,128)} fusion(f32[4,512,512]{2,1,0:T(8,128)} %copy-done, bf16[512,4,2,128]{3,0,1,2:T(8,128)(2,1)} %get-tuple-element.387, bf16[512,4,2,128]{3,0,1,2:T(8,128)(2,1)S(1)} %dynamic-slice_bitcast_fusion.2), kind=kOutput, calls=%fused_computation.45 | convolution fusion | flops 547618816 | bytes 6815744 | tf_op jit(solution)/shard_map/while/body/eval_jaxpr/cond/branch_1_fun/hac,ahd->chd/dot_general | solution.py:47
  270.0 2.0 maximum_add_fusion
  272.1 1.6 copy.77
  273.7 1.3 convert_bitcast_fusion
  275.8 4.5 %maximum_bitcast_fusion = bf16[1,512,4,4,128]{4,3,2,1,0:T(4,128)(2,1)} fusion(bf16[512,4,2,128]{3,2,1,0:T(2,128)(2,1)S(1)} %copy.77, bf16[512,4,1,128]{3,2,1,0:T(2,128)(2,1)S(1)} %copy.51, bf16[512,4,1,128]{3,2,1,0:T(2,128)(2,1)S(1)} %copy-done.8), kind=kLoop, calls=%fused_computation.67 | loop fusion | flops 6291456 | bytes 4194304 | tf_op jit(solution)/shard_map/broadcast_in_dim | solution.py:206
  (86 shorter events, 15.5 us)
Async XLA Ops:
  7.2 7.0 %copy-start.14 = (s32[1,4,3]{1,0,2:T(1,128)S(1)}, s32[1,4,3]{1,0,2:T(1,128)}, u32[]{:S(2)}) copy-start(s32[1,4,3]{1,0,2:T(1,128)} %param.21) | copy-start | bytes 148
  7.2 8.6 %copy-start.13 = (f32[1,2048]{1,0:T(1,128)S(1)}, f32[1,2048]{1,0:T(1,128)}, u32[]{:S(2)}) copy-start(f32[1,2048]{1,0:T(1,128)} %param.18) | copy-start | bytes 24580
  7.2 9.3 %copy-start.12 = (s32[1,2048]{1,0:T(1,128)S(1)}, s32[1,2048]{1,0:T(1,128)}, u32[]{:S(2)}) copy-start(s32[1,2048]{1,0:T(1,128)} %param.19) | copy-start | bytes 24580
  7.2 10.1 %copy-start.15 = (s32[1,2048]{1,0:T(1,128)S(1)}, s32[1,2048]{1,0:T(1,128)}, u32[]{:S(2)}) copy-start(s32[1,2048]{1,0:T(1,128)} %param.20) | copy-start | bytes 24580
  7.2 98.5 %all-gather.2.cloned.1.call-start = ((), (), s32[]{:S(2)}) async-start(), calls=%async_computation | async-start | bytes 5242880 | tf_op jit(solution)/shard_map/all_gather | solution.py:98
  9.4 60.7 %copy-start.2 = (bf16[1,512,4,4,128]{4,1,2,3,0:T(8,128)(2,1)}, bf16[1,512,4,4,128]{4,1,2,3,0:T(8,128)(2,1)S(1)}, u32[]{:S(2)}) copy-start(bf16[1,512,4,4,128]{4,1,2,3,0:T(8,128)(2,1)S(1)} %copy.78) | copy-start | bytes 6291460
  10.6 59.5 %collective-permute-start = (bf16[512,4,2,128]{3,0,1,2:T(8,128)(2,1)}, bf16[512,4,2,128]{3,0,1,2:T(8,128)(2,1)}, u32[]{:S(2)}, u32[]{:S(2)}) collective-permute-start(bf16[512,4,2,128]{3,0,1,2:T(8,128)(2,1)} %slice.88), channel_id=1, source_target_pairs={{0,4},{4,8},{8,12},{1,5},{5,9},{9,13},{2,6},{6,10},{10,14},{3,7},{... | collective-permute-start | bytes 3145736 | tf_op jit(solution)/shard_map/ppermute | solution.py:24
  17.7 52.3 %copy-start.10 = (pred[512,512]{1,0:T(8,128)(4,1)}, pred[512,512]{1,0:T(8,128)(4,1)S(1)}, u32[]{:S(2)}) copy-start(pred[512,512]{1,0:T(8,128)(4,1)S(1)} %get-tuple-element.483) | copy-start | bytes 786436
  21.3 53.3 %copy-start.4 = (bf16[4,512,512]{2,1,0:T(8,128)(2,1)}, bf16[4,512,512]{2,1,0:T(8,128)(2,1)S(1)}, u32[]{:S(2)}) copy-start(bf16[4,512,512]{2,1,0:T(8,128)(2,1)S(1)} %get-tuple-element.485) | copy-start | bytes 6291460
  74.6 1.3 copy-start.6
  110.3 5.8 %copy-start.9 = (bf16[1,512,4,128]{3,2,1,0:T(4,128)(2,1)S(1)}, bf16[1,512,4,128]{3,2,1,0:T(4,128)(2,1)}, u32[]{:S(2)}) copy-start(bf16[1,512,4,128]{3,2,1,0:T(4,128)(2,1)} %param.17) | copy-start | bytes 1572868
  115.1 50.9 %copy-start.1 = (bf16[512,4,1,128]{3,0,1,2:T(8,128)(2,1)}, bf16[512,4,1,128]{3,0,1,2:T(8,128)(2,1)S(1)}, u32[]{:S(2)}) copy-start(bf16[512,4,1,128]{3,0,1,2:T(8,128)(2,1)S(1)} %get-tuple-element.648) | copy-start | bytes 1572868
  115.5 6.2 %copy-start.7 = (bf16[4,512,512]{2,1,0:T(8,128)(2,1)S(1)}, bf16[4,512,512]{2,1,0:T(8,128)(2,1)}, u32[]{:S(2)}) copy-start(bf16[4,512,512]{2,1,0:T(8,128)(2,1)} %copy-done.6) | copy-start | bytes 6291460
  116.1 6.4 %copy-start.11 = (pred[512,512]{1,0:T(8,128)(4,1)S(1)}, pred[512,512]{1,0:T(8,128)(4,1)}, u32[]{:S(2)}) copy-start(pred[512,512]{1,0:T(8,128)(4,1)} %copy-done.10) | copy-start | bytes 786436
  116.2 6.4 %copy-start.17 = (f32[4,512,512]{2,1,0:T(8,128)S(1)}, f32[4,512,512]{2,1,0:T(8,128)}, u32[]{:S(2)}) copy-start(f32[4,512,512]{2,1,0:T(8,128)} %get-tuple-element.488) | copy-start | bytes 12582916
  122.6 3.3 %copy-start.3 = (bf16[1,512,4,4,128]{4,1,2,3,0:T(8,128)(2,1)S(1)}, bf16[1,512,4,4,128]{4,1,2,3,0:T(8,128)(2,1)}, u32[]{:S(2)}) copy-start(bf16[1,512,4,4,128]{4,1,2,3,0:T(8,128)(2,1)} %copy-done.2) | copy-start | bytes 6291460
  125.9 5.4 %copy-start.16 = (f32[4,512,512]{2,1,0:T(8,128)S(1)}, f32[4,512,512]{2,1,0:T(8,128)}, u32[]{:S(2)}) copy-start(f32[4,512,512]{2,1,0:T(8,128)} %get-tuple-element.486) | copy-start | bytes 12582916
  127.0 25.2 %collective-permute-start.2 = (bf16[512,4,2,128]{3,0,1,2:T(8,128)(2,1)S(1)}, bf16[512,4,2,128]{3,0,1,2:T(8,128)(2,1)S(1)}, u32[]{:S(2)}, u32[]{:S(2)}) collective-permute-start(bf16[512,4,2,128]{3,0,1,2:T(8,128)(2,1)S(1)} %pad_maximum_fusion.1), channel_id=1, source_target_pairs={{0,4},{4,8},{8,12},{12,0},{1,5},{5,9},{9,13},{13,1},{2,6},{6,10},{... | collective-permute-start | bytes 3145736 | tf_op jit(solution)/shard_map/ppermute | solution.py:16
  129.5 55.8 %collective-permute-start.1 = (bf16[512,4,2,128]{3,0,1,2:T(8,128)(2,1)S(1)}, bf16[512,4,2,128]{3,0,1,2:T(8,128)(2,1)S(1)}, u32[]{:S(2)}, u32[]{:S(2)}) collective-permute-start(bf16[512,4,2,128]{3,0,1,2:T(8,128)(2,1)S(1)} %pad_maximum_fusion), channel_id=1, source_target_pairs={{4,0},{8,4},{12,8},{5,1},{9,5},{13,9},{6,2},{10,6},{14,10},{7,3},{... | collective-permute-start | bytes 3145736 | tf_op jit(solution)/shard_map/ppermute | solution.py:24
  152.2 32.0 %collective-permute-start.3 = (bf16[512,4,2,128]{3,0,1,2:T(8,128)(2,1)S(1)}, bf16[512,4,2,128]{3,0,1,2:T(8,128)(2,1)S(1)}, u32[]{:S(2)}, u32[]{:S(2)}) collective-permute-start(bf16[512,4,2,128]{3,0,1,2:T(8,128)(2,1)S(1)} %collective-permute-done.2), channel_id=1, source_target_pairs={{0,4},{4,8},{8,12},{12,0},{1,5},{5,9},{9,13},{13,1},{2,6},{6,10},{... | collective-permute-start | bytes 3145736 | tf_op jit(solution)/shard_map/ppermute | solution.py:16
  166.0 18.2 %copy-start.5 = (bf16[4,512,512]{2,1,0:T(8,128)(2,1)S(1)}, bf16[4,512,512]{2,1,0:T(8,128)(2,1)}, u32[]{:S(2)}) copy-start(bf16[4,512,512]{2,1,0:T(8,128)(2,1)} %copy-done.4) | copy-start | bytes 6291460
  184.2 44.9 %collective-permute-start.4 = (bf16[512,4,2,128]{3,0,1,2:T(8,128)(2,1)S(1)}, bf16[512,4,2,128]{3,0,1,2:T(8,128)(2,1)S(1)}, u32[]{:S(2)}, u32[]{:S(2)}) collective-permute-start(bf16[512,4,2,128]{3,0,1,2:T(8,128)(2,1)S(1)} %collective-permute-done.3), channel_id=1, source_target_pairs={{0,4},{4,8},{8,12},{12,0},{1,5},{5,9},{9,13},{13,1},{2,6},{6,10},{... | collective-permute-start | bytes 3145736 | tf_op jit(solution)/shard_map/ppermute | solution.py:16
  242.1 2.0 copy-start
  259.8 2.0 copy-start
  272.1 3.8 %copy-start.8 = (bf16[512,4,1,128]{3,2,1,0:T(2,128)(2,1)S(1)}, bf16[512,4,1,128]{3,2,1,0:T(2,128)(2,1)}, u32[]{:S(2)}) copy-start(bf16[512,4,1,128]{3,2,1,0:T(2,128)(2,1)} %copy.50) | copy-start | bytes 1572868
Sparse Core Ops, SparseCore 0:
  10.7 94.9 all-gather.1
